TPU v7x, 256 devices: a whole 4x4x8 slice. The times are simulated.
256 devices in a mesh: pipe: 16 (over y, x_lo, core), fsdp: 8 (over z), tp: 2 (over x_hi).
Axes of the slice: x: 4 (x_hi: 2, x_lo: 2; x = x_hi * 2 + x_lo), y: 4, z: 8, core: 2. Of those that a mesh axis runs over, the one named last changes fastest.
Arguments:
- act_in: bfloat16 [16, 2, 8, 128, 4096], P('pipe', None, 'fsdp', None, 'tp'), may hold values from -6 to 6
- gate_q: bfloat16 [16, 2, 8, 128, 4096], P('pipe', None, 'fsdp', None, 'tp'), may hold values from -6 to 6
- gate_k: bfloat16 [16, 2, 8, 128, 4096], P('pipe', None, 'fsdp', None, 'tp'), may hold values from -6 to 6
- grad_in: bfloat16 [16, 8, 128, 4096], P('pipe', 'fsdp', None, 'tp'), may hold values from -6 to 6
- weight: bfloat16 [16, 4096, 4096], P('pipe', 'tp', 'fsdp'), may hold values from -0.09375 to 0.09375
- filters: bfloat16 [16, 128, 256], P('pipe', None, 'tp'), may hold values from -0.5 to 0.5
Outputs:
- grad_out: bfloat16 [16, 2, 8, 128, 4096], P('pipe', None, 'fsdp', None, 'tp')
- filter_grad: float32 [16, 128, 256], P('pipe', 'fsdp', 'tp')
All inputs are finite; a program needn't handle non-finite values.
Results may differ from a plain program's by a relative error of at most 0.0056.
Values may be sent and summed in bfloat16 or wider, within the bound.
No kernel may reach another device: no remote copies, remote signals or barrier semaphores. Data moves between devices by JAX's collectives and lax.ppermute only.
A program may use at most 128 MiB of HBM per device.

v0:
```python
import math
import jax
import jax.numpy as jnp
from jax import lax
from jax.sharding import PartitionSpec as P


def passed_along(value, axis, by):
    peers = lax.axis_size(axis)
    pairs = [(i, i + by) for i in range(peers) if 0 <= i + by < peers]
    return lax.ppermute(value, axis, pairs)


def toeplitz(taps_table, seqlen):
    rows = taps_table.T
    padded = jnp.pad(rows, ((0, 0), (0, 2 * seqlen - rows.shape[1])))
    tiled = jnp.tile(padded, (1, seqlen))
    cut = tiled[:, : seqlen * (2 * seqlen - 1)].reshape(rows.shape[0], seqlen, 2 * seqlen - 1)
    return cut[:, :, :seqlen]


def filter_terms(adjoint, shaped, taps):
    seqlen = adjoint.shape[0]
    groups_loc = adjoint.shape[1]
    flipped = jnp.pad(shaped[::-1], ((0, taps), (0, 0), (0, 0)))
    span = seqlen + taps
    block = math.gcd(groups_loc, 16)
    pieces = []
    for first in range(0, groups_loc, block):
        corr = jnp.einsum(
            "tgc,ugc->gtu",
            adjoint[:, first : first + block],
            flipped[:, first : first + block],
            preferred_element_type=jnp.float32,
        )
        flat = corr.reshape(block, seqlen * span)[:, : seqlen * (span - 1)]
        skewed = flat.reshape(block, seqlen, span - 1)[:, :, seqlen - 1 : seqlen - 1 + taps]
        pieces.append(jnp.sum(skewed, axis=1))
    return jnp.concatenate(pieces, axis=0).T


def body(act_in, gate_q, gate_k, grad_in, weight, filters):
    ticks = act_in.shape[1]
    seqlen = act_in.shape[3]
    width_loc = act_in.shape[4]
    taps = filters.shape[1]
    groups_loc = filters.shape[2]
    per_group = width_loc // groups_loc
    scale = 1.0 / math.sqrt(ticks * lax.axis_size("fsdp") * seqlen * per_group)
    kernel = toeplitz(filters[0], seqlen)
    contract = (((1,), (1,)), ((), ()))
    incoming = grad_in[0, 0]
    outputs = []
    pending = jnp.zeros((taps, groups_loc), jnp.float32)
    for tick in range(ticks):
        if tick > 0:
            incoming = passed_along(outputs[-1], "pipe", -1)
        whole = lax.all_gather(incoming, "tp", axis=1, tiled=True)

        def add_panel(total, piece, start, whole=whole):
            return lax.dot_general(whole, piece, contract, preferred_element_type=jnp.float32)

        deriv = add_panel(
            jnp.zeros((seqlen, width_loc), jnp.float32),
            lax.all_gather(weight[0], "fsdp", axis=1, tiled=True),
            jnp.int32(0),
        )
        adjoint = (
            (gate_q[0, tick, 0] * deriv).astype(jnp.bfloat16).reshape(seqlen, groups_loc, per_group)
        )
        back = jnp.einsum(
            "gtu,ugc->tgc", kernel, adjoint, preferred_element_type=jnp.float32
        ).reshape(seqlen, width_loc)
        result = (incoming + gate_k[0, tick, 0] * back).astype(jnp.bfloat16)
        outputs.append(result)
        shaped = (
            gate_k[0, tick, 0].astype(jnp.float32) * act_in[0, tick, 0].astype(jnp.float32)
        ).astype(jnp.bfloat16)
        term = filter_terms(adjoint, shaped.reshape(seqlen, groups_loc, per_group), taps) * scale
        pending = pending + term
    summed = lax.psum_scatter(pending, "fsdp", scatter_dimension=0, tiled=True)
    grads = jnp.stack(outputs, axis=0)[None, :, None]
    return (grads, summed[None])


def solution(mesh):
    placed = (
        P("pipe", None, "fsdp", None, "tp"),
        P("pipe", None, "fsdp", None, "tp"),
        P("pipe", None, "fsdp", None, "tp"),
        P("pipe", "fsdp", None, "tp"),
        P("pipe", "tp", "fsdp"),
        P("pipe", None, "tp"),
    )
    return jax.shard_map(
        body,
        mesh=mesh,
        in_specs=placed,
        out_specs=(P("pipe", None, "fsdp", None, "tp"), P("pipe", "fsdp", "tp")),
        check_vma=False,
    )
```

profile of v0, /device:TPU:2, one launch (start us, length us, event | category | flops | bytes accessed | tf_op | source)
XLA Modules:
  0.0 514.4 jit_solution(2104143820232488051)
XLA Ops:
  8.9 3.8 tile.4
  12.7 12.3 %copy.61 = bf16[16,8,128,256]{3,1,2,0:T(8,128)(2,1)} copy(bf16[16,8,128,256]{3,2,1,0:T(8,128)(2,1)} %bitcast.136) | data formatting | bytes 16777216
  25.0 7.4 %slice.290 = bf16[128,32640]{1,0:T(8,128)(2,1)} slice(bf16[128,32768]{1,0:T(8,128)(2,1)} %bitcast.137), slice={[0:128], [0:32640]} | slice | bytes 16711680 | tf_op jit(solution)/shard_map/slice | solution.py:18
  32.4 29.8 %reshape.184 = bf16[128,128,255]{2,1,0:T(8,128)(2,1)} reshape(bf16[128,32640]{1,0:T(8,128)(2,1)} %slice.290) | data formatting | bytes 16711680 | tf_op jit(solution)/shard_map/reshape | solution.py:18
  64.0 150.7 %all-gather.10.cloned.1.call-done = bf16[1,2048,4096]{2,1,0:T(8,128)(2,1)} async-done(((bf16[1,2048,512]{2,1,0:T(8,128)(2,1)}), bf16[1,2048,4096]{2,1,0:T(8,128)(2,1)}) %all-gather.10.cloned.1.call-update) | async-done | bytes 16777232 | tf_op jit(solution)/shard_map/all_gather | solution.py:65
  214.7 11.8 %fusion.17 = bf16[128,2048]{1,0:T(8,128)(2,1)S(1)} fusion(bf16[1,2048,4096]{2,1,0:T(8,128)(2,1)} %all-gather.10.cloned.1.call-done, bf16[1,1,128,4096]{3,2,1,0:T(8,128)(2,1)} %all-gather.8.cloned.1.call-done, bf16[1,2,1,128,2048]{4,3,2,1,0:T(8,128)(2,1)S(1)} %copy-done.9), kind=kOutput, calls=%fused_computation.11 | convolution fusion | flops 2148270080 | bytes 18874368 | tf_op jit(solution)/shard_map/dot_general | solution.py:61
  247.9 6.2 %reshape.190 = f32[16,128,255]{2,1,0:T(8,128)} reshape(f32[16,32640]{1,0:T(8,128)} %slice.292) | data formatting | bytes 4177920 | tf_op jit(solution)/shard_map/reshape | solution.py:37
  256.1 2.8 copy.63
  260.4 6.1 %reshape.192 = f32[16,128,255]{2,1,0:T(8,128)} reshape(f32[16,32640]{1,0:T(8,128)} %slice.294) | data formatting | bytes 4177920 | tf_op jit(solution)/shard_map/reshape | solution.py:37
  272.7 6.1 %reshape.194 = f32[16,128,255]{2,1,0:T(8,128)} reshape(f32[16,32640]{1,0:T(8,128)} %slice.296) | data formatting | bytes 4177920 | tf_op jit(solution)/shard_map/reshape | solution.py:37
  280.8 3.2 copy.65
  285.5 6.1 %reshape.196 = f32[16,128,255]{2,1,0:T(8,128)} reshape(f32[16,32640]{1,0:T(8,128)} %slice.298) | data formatting | bytes 4177920 | tf_op jit(solution)/shard_map/reshape | solution.py:37
  297.8 6.3 %reshape.198 = f32[16,128,255]{2,1,0:T(8,128)} reshape(f32[16,32640]{1,0:T(8,128)} %slice.300) | data formatting | bytes 4177920 | tf_op jit(solution)/shard_map/reshape | solution.py:37
  310.3 6.1 %reshape.200 = f32[16,128,255]{2,1,0:T(8,128)} reshape(f32[16,32640]{1,0:T(8,128)} %slice.302) | data formatting | bytes 4177920 | tf_op jit(solution)/shard_map/reshape | solution.py:37
  326.3 6.2 %reshape.202 = f32[16,128,255]{2,1,0:T(8,128)} reshape(f32[16,32640]{1,0:T(8,128)} %slice.304) | data formatting | bytes 4177920 | tf_op jit(solution)/shard_map/reshape | solution.py:37
  332.5 3.0 copy.69
  336.9 6.1 %reshape.204 = f32[16,128,255]{2,1,0:T(8,128)} reshape(f32[16,32640]{1,0:T(8,128)} %slice.306) | data formatting | bytes 4177920 | tf_op jit(solution)/shard_map/reshape | solution.py:37
  349.5 12.0 %fusion.14 = bf16[128,2048]{1,0:T(8,128)(2,1)S(1)} fusion(bf16[128,4096]{1,0:T(8,128)(2,1)} %all-gather.6.cloned.1.call-done, bf16[1,2048,4096]{2,1,0:T(8,128)(2,1)} %all-gather.10.cloned.1.call-done, bf16[1,2,1,128,2048]{4,3,2,1,0:T(8,128)(2,1)} %param.7), kind=kOutput, calls=%fused_computation.10 | convolution fusion | flops 2148270080 | bytes 18874368 | tf_op jit(solution)/shard_map/dot_general | solution.py:61
  372.6 3.3 fusion.4
  378.6 6.2 %reshape.206 = f32[16,128,255]{2,1,0:T(8,128)} reshape(f32[16,32640]{1,0:T(8,128)} %slice.308) | data formatting | bytes 4177920 | tf_op jit(solution)/shard_map/reshape | solution.py:37
  386.8 2.8 copy.71
  391.1 6.1 %reshape.208 = f32[16,128,255]{2,1,0:T(8,128)} reshape(f32[16,32640]{1,0:T(8,128)} %slice.310) | data formatting | bytes 4177920 | tf_op jit(solution)/shard_map/reshape | solution.py:37
  399.2 3.2 copy.72
  403.8 6.2 %reshape.210 = f32[16,128,255]{2,1,0:T(8,128)} reshape(f32[16,32640]{1,0:T(8,128)} %slice.312) | data formatting | bytes 4177920 | tf_op jit(solution)/shard_map/reshape | solution.py:37
  411.9 2.8 copy.73
  416.2 6.2 %reshape.212 = f32[16,128,255]{2,1,0:T(8,128)} reshape(f32[16,32640]{1,0:T(8,128)} %slice.314) | data formatting | bytes 4177920 | tf_op jit(solution)/shard_map/reshape | solution.py:37
  428.6 6.2 %reshape.214 = f32[16,128,255]{2,1,0:T(8,128)} reshape(f32[16,32640]{1,0:T(8,128)} %slice.316) | data formatting | bytes 4177920 | tf_op jit(solution)/shard_map/reshape | solution.py:37
  436.7 3.0 copy.75
  441.1 6.2 %reshape.216 = f32[16,128,255]{2,1,0:T(8,128)} reshape(f32[16,32640]{1,0:T(8,128)} %slice.318) | data formatting | bytes 4177920 | tf_op jit(solution)/shard_map/reshape | solution.py:37
  453.5 6.2 %reshape.218 = f32[16,128,255]{2,1,0:T(8,128)} reshape(f32[16,32640]{1,0:T(8,128)} %slice.320) | data formatting | bytes 4177920 | tf_op jit(solution)/shard_map/reshape | solution.py:37
  463.0 4.6 reshape.220
  473.2 32.9 %reduce-scatter.4.cloned.1.call-done = f32[16,128]{1,0:T(8,128)} async-done(((f32[128,128]{1,0:T(8,128)}), f32[16,128]{1,0:T(8,128)}) %reduce-scatter.4.cloned.1.call-update) | async-done | bytes 8208
  (137 shorter events, 117.9 us)
Async XLA Ops:
  7.2 1.5 copy-start.10
  7.2 56.8 %all-gather.8.cloned.1.call-start = ((), (), s32[]{:S(2)}) async-start(), calls=%async_computation.2 | async-start | bytes 1572864 | tf_op jit(solution)/shard_map/all_gather | solution.py:58
  7.9 206.8 %all-gather.10.cloned.1.call-start = ((), (), s32[]{:S(2)}) async-start(), calls=%async_computation.3 | async-start | bytes 18874368 | tf_op jit(solution)/shard_map/all_gather | solution.py:65
  8.7 340.8 %all-gather.6.cloned.1.call-start = ((), (), s32[]{:S(2)}) async-start(), calls=%async_computation.1 | async-start | bytes 1572864 | tf_op jit(solution)/shard_map/all_gather | solution.py:58
  32.4 29.8 %copy-start.1 = (bf16[1,2,1,128,2048]{4,3,2,1,0:T(8,128)(2,1)S(1)}, bf16[1,2,1,128,2048]{4,3,2,1,0:T(8,128)(2,1)}, u32[]{:S(2)}) copy-start(bf16[1,2,1,128,2048]{4,3,2,1,0:T(8,128)(2,1)} %param.8) | copy-start | bytes 3145732
  32.4 29.8 %copy-start.8 = (bf16[1,2,1,128,2048]{4,3,2,1,0:T(8,128)(2,1)S(1)}, bf16[1,2,1,128,2048]{4,3,2,1,0:T(8,128)(2,1)}, u32[]{:S(2)}) copy-start(bf16[1,2,1,128,2048]{4,3,2,1,0:T(8,128)(2,1)} %param.6) | copy-start | bytes 3145732
  62.6 152.1 %copy-start.9 = (bf16[1,2,1,128,2048]{4,3,2,1,0:T(8,128)(2,1)S(1)}, bf16[1,2,1,128,2048]{4,3,2,1,0:T(8,128)(2,1)}, u32[]{:S(2)}) copy-start(bf16[1,2,1,128,2048]{4,3,2,1,0:T(8,128)(2,1)} %param.7) | copy-start | bytes 3145732
  226.8 10.2 %slice-start = ((s8[8388608]{0:T(1024)(128)(4,1)}), s8[4194304]{0:T(1024)(128)(4,1)S(1)}, s32[]{:S(2)}) async-start(s8[8388608]{0:T(1024)(128)(4,1)} %bitcast.132), calls=%async_computation.5 | async-start | bytes 8388608
  231.8 5.1 slice-start.1
  239.2 1.3 copy-start.4
  240.5 4.7 copy-start
  243.1 78.7 %collective-permute-start = (bf16[128,2048]{1,0:T(8,128)(2,1)}, bf16[128,2048]{1,0:T(8,128)(2,1)}, u32[]{:S(2)}, u32[]{:S(2)}) collective-permute-start(bf16[128,2048]{1,0:T(8,128)(2,1)} %fusion.23), channel_id=1, source_target_pairs={{16,0},{32,16},{48,32},{64,48},{80,64},{96,80},{112,96},{128,112},... | collective-permute-start | bytes 1572872 | tf_op jit(solution)/shard_map/ppermute | solution.py:11
  321.8 184.3 %reduce-scatter.4.cloned.1.call-start = ((), (), s32[]{:S(2)}) async-start(), calls=%async_computation.4 | async-start | bytes 73728
  343.1 5.3 %copy-start.2 = (bf16[1,2,1,128,2048]{4,3,2,1,0:T(8,128)(2,1)S(1)}, bf16[1,2,1,128,2048]{4,3,2,1,0:T(8,128)(2,1)}, u32[]{:S(2)}) copy-start(bf16[1,2,1,128,2048]{4,3,2,1,0:T(8,128)(2,1)} %param.8) | copy-start | bytes 3145732
  344.4 4.0 copy-start.5
  363.7 8.8 %slice-start.2 = ((s8[8388608]{0:T(1024)(128)(4,1)}), s8[4194304]{0:T(1024)(128)(4,1)S(1)}, s32[]{:S(2)}) async-start(s8[8388608]{0:T(1024)(128)(4,1)} %bitcast.134), calls=%async_computation.7 | async-start | bytes 8388608
  368.8 3.8 slice-start.3
  463.0 7.5 %copy-start.6 = (f32[128,16,128]{2,1,0:T(8,128)S(1)}, f32[128,16,128]{2,1,0:T(8,128)}, u32[]{:S(2)}) copy-start(f32[128,16,128]{2,1,0:T(8,128)} %fusion.4) | copy-start | bytes 3145732
  467.6 3.2 copy-start.3
  470.8 1.3 copy-start.7
Sparse Core Ops, SparseCore 0:
  9.8 29.9 all-gather.7
  41.6 173.1 all-gather.9
  322.0 26.2 all-gather.5
  470.6 35.5 reduce-scatter.3
where the time goes:
time: 522 us; the launch traced here: 514 us
  local copies, waits for them, and re-layouts  221 us (42%)
  waiting for transfers between devices  185 us (35%)
  matrix products  53.6 us (10%)
  other arithmetic  37.5 us (7%)
  between operations  14.5 us (3%)
    all_gather x1, waiting for transfers between devices, body(): lax.all_gather(weight[0], 'fsdp', axis=1, tiled=True)  151 us
    reshape x16, local copies, waits for them, and re-layouts, filter_terms(): flat.reshape(block, seqlen, span - 1)[:, :, seqlen - 1:seqlen - 1 + taps]  97.1 us
    unnamed x65, local copies, waits for them, and re-layouts  56 us
    unnamed x5, waiting for transfers between devices  34.4 us
    reduce_sum x16, other arithmetic, filter_terms(): pieces.append(jnp.sum(skewed, axis=1))  31.1 us
    reshape x1, local copies, waits for them, and re-layouts, toeplitz(): tiled[:, :seqlen * (2 * seqlen - 1)]  29.8 us
    dot_general x16, matrix products, filter_terms(): jnp.einsum('tgc,ugc->gtu', adjoint[:, first:first + block], flipped[:, fi...  24.3 us
    dot_general x2, matrix products, add_panel(): lax.dot_general(whole, piece, contract, preferred_element_type=jnp.float32)  23.7 us
  transfers between devices with their start and end apart: 5, of which 2 were waited for; matrix products, arithmetic and copies ran while one was open for 31% of the time, Pallas kernels for 0%

commit v1 on v0

--- a/solution.py
+++ b/solution.py
@@ -3,6 +3,12 @@
 import jax.numpy as jnp
 from jax import lax
 from jax.sharding import PartitionSpec as P
+
+
+def _create_steps_all(block_here, ndim_at):
+    block_last = list(block_here.shape[1:])
+    block_last[ndim_at] *= block_here.shape[0]
+    return jnp.moveaxis(block_here, 0, ndim_at).reshape(block_last)
 
 
 def passed_along(value, axis, by):
@@ -60,9 +66,26 @@
         def add_panel(total, piece, start, whole=whole):
             return lax.dot_general(whole, piece, contract, preferred_element_type=jnp.float32)
 
+        def _solve_outputs(slab_in, mesh_ax, d_out):
+            n_dev_all = lax.axis_size(mesh_ax)
+            store = [(dev, (dev + 1) % n_dev_all) for dev in range(n_dev_all)]
+            leaves = [(h, dev_j) for dev_j, h in store]
+            mid_arr, e_next = ([], [])
+            for at in range(n_dev_all - 1):
+                if at % 2 == 0:
+                    mid_arr.append(
+                        lax.ppermute(mid_arr[-1] if mid_arr else slab_in, mesh_ax, store)
+                    )
+                else:
+                    e_next.append(lax.ppermute(e_next[-1] if e_next else slab_in, mesh_ax, leaves))
+            n_now = jnp.stack([*mid_arr[::-1], slab_in, *e_next], axis=0)
+            t_next = lax.axis_index(mesh_ax) - len(mid_arr)
+            n_now = n_now[(jnp.arange(n_dev_all) - t_next) % n_dev_all]
+            return _create_steps_all(n_now, d_out)
+
         deriv = add_panel(
             jnp.zeros((seqlen, width_loc), jnp.float32),
-            lax.all_gather(weight[0], "fsdp", axis=1, tiled=True),
+            _solve_outputs(weight[0], "fsdp", 1),
             jnp.int32(0),
         )
         adjoint = (

time: 522 us -> 625 us (1.20)
  local copies, waits for them, and re-layouts: 221 us -> 281 us
  waiting for transfers between devices: 185 us -> 206 us
  other arithmetic: 37.5 us -> 53.1 us
  starting transfers between devices: 2.45 us -> 15 us
    ppermute x0 -> x7, waiting for transfers between devices: none -> 172 us  [the longest x4 139 us: _solve_outputs(): lax.ppermute(mid_arr[-1] if mid_arr else slab_in, mesh_ax, store)]
    all_gather x1 -> x0, waiting for transfers between devices: 151 us -> none  [body(): lax.all_gather(weight[0], 'fsdp', axis=1, tiled=True)]
    gather x0 -> x3, local copies, waits for them, and re-layouts: none -> 22.1 us  [_solve_outputs(): n_now = n_now[(jnp.arange(n_dev_all) - t_next) % n_dev_all]]
    transpose x0 -> x1, local copies, waits for them, and re-layouts: none -> 21.6 us  [_create_steps_all(): return jnp.moveaxis(block_here, 0, ndim_at).reshape(block_last)]
    transpose x0 -> x1, other arithmetic: none -> 13.6 us  [_create_steps_all(): return jnp.moveaxis(block_here, 0, ndim_at).reshape(block_last)]
    ppermute x0 -> x7, starting transfers between devices: none -> 12.2 us  [the longest x3 10.2 us: _solve_outputs(): lax.ppermute(e_next[-1] if e_next else slab_in, mesh_ax, leaves)]
    unnamed x65 -> x81, local copies, waits for them, and re-layouts: 56 us -> 67.6 us
    unnamed x5 -> x4, waiting for transfers between devices: 34.4 us -> 34 us
  transfers between devices with their start and end apart: 5 -> 11, of which waited for: 2 -> 5; matrix products, arithmetic and copies ran while one was open for 31% -> 38% of each run, Pallas kernels for 0% -> 0%
where the time goes in v1:
time: 625 us; the launch traced here: 619 us
  local copies, waits for them, and re-layouts  281 us (45%)
  waiting for transfers between devices  206 us (33%)
  other arithmetic  53.1 us (8%)
  matrix products  49.2 us (8%)
  starting transfers between devices  15 us (2%)
  between operations  14.8 us (2%)
    ppermute x4, waiting for transfers between devices, _solve_outputs(): lax.ppermute(mid_arr[-1] if mid_arr else slab_in, mesh_ax, store)  139 us
    reshape x16, local copies, waits for them, and re-layouts, filter_terms(): flat.reshape(block, seqlen, span - 1)[:, :, seqlen - 1:seqlen - 1 + taps]  97.5 us
    unnamed x81, local copies, waits for them, and re-layouts  67.6 us
    unnamed x4, waiting for transfers between devices  34 us
    ppermute x3, waiting for transfers between devices, _solve_outputs(): lax.ppermute(e_next[-1] if e_next else slab_in, mesh_ax, leaves)  33.2 us
    reduce_sum x16, other arithmetic, filter_terms(): pieces.append(jnp.sum(skewed, axis=1))  31.1 us
    reshape x1, local copies, waits for them, and re-layouts, toeplitz(): tiled[:, :seqlen * (2 * seqlen - 1)]  29.5 us
    dot_general x16, matrix products, filter_terms(): jnp.einsum('tgc,ugc->gtu', adjoint[:, first:first + block], flipped[:, fi...  24.5 us
  transfers between devices with their start and end apart: 11, of which 5 were waited for; matrix products, arithmetic and copies ran while one was open for 38% of the time, Pallas kernels for 0%

profile of v1, /device:TPU:2, one launch (start us, length us, event | category | flops | bytes accessed | tf_op | source)
XLA Modules:
  0.0 618.8 jit_solution(3314686142730985370)
XLA Ops:
  9.2 49.8 %collective-permute-done = bf16[2048,512]{1,0:T(8,128)(2,1)S(1)} collective-permute-done((bf16[2048,512]{1,0:T(8,128)(2,1)}, bf16[2048,512]{1,0:T(8,128)(2,1)S(1)}, u32[]{:S(2)}, u32[]{:S(2)}) %collective-permute-start) | collective-permute-done | bytes 2097184 | tf_op jit(solution)/shard_map/ppermute | solution.py:77
  62.2 44.8 %collective-permute-done.1 = bf16[2048,512]{1,0:T(8,128)(2,1)S(1)} collective-permute-done((bf16[2048,512]{1,0:T(8,128)(2,1)S(1)}, bf16[2048,512]{1,0:T(8,128)(2,1)S(1)}, u32[]{:S(2)}, u32[]{:S(2)}) %collective-permute-start.1) | collective-permute-done | bytes 2097184 | tf_op jit(solution)/shard_map/ppermute | solution.py:77
  111.6 44.0 %collective-permute-done.2 = bf16[2048,512]{1,0:T(8,128)(2,1)} collective-permute-done((bf16[2048,512]{1,0:T(8,128)(2,1)S(1)}, bf16[2048,512]{1,0:T(8,128)(2,1)}, u32[]{:S(2)}, u32[]{:S(2)}) %collective-permute-start.2) | collective-permute-done | bytes 2097184 | tf_op jit(solution)/shard_map/ppermute | solution.py:77
  158.0 3.8 tile.4
  161.8 12.3 %copy.65 = bf16[16,8,128,256]{3,1,2,0:T(8,128)(2,1)} copy(bf16[16,8,128,256]{3,2,1,0:T(8,128)(2,1)} %bitcast.153) | data formatting | bytes 16777216
  174.2 7.1 %slice.294 = bf16[128,32640]{1,0:T(8,128)(2,1)} slice(bf16[128,32768]{1,0:T(8,128)(2,1)} %bitcast.154), slice={[0:128], [0:32640]} | slice | bytes 16711680 | tf_op jit(solution)/shard_map/slice | solution.py:24
  181.3 29.5 %reshape.238 = bf16[128,128,255]{2,1,0:T(8,128)(2,1)} reshape(bf16[128,32640]{1,0:T(8,128)(2,1)} %slice.294) | data formatting | bytes 16711680 | tf_op jit(solution)/shard_map/reshape | solution.py:24
  231.6 33.2 %collective-permute-done.6 = bf16[2048,512]{1,0:T(8,128)(2,1)S(1)} collective-permute-done((bf16[2048,512]{1,0:T(8,128)(2,1)}, bf16[2048,512]{1,0:T(8,128)(2,1)S(1)}, u32[]{:S(2)}, u32[]{:S(2)}) %collective-permute-start.6) | collective-permute-done | bytes 2097184 | tf_op jit(solution)/shard_map/ppermute | solution.py:80
  264.9 6.0 fusion.54
  270.9 8.1 %gather_fusion = bf16[8,1024,512]{2,1,0:T(8,128)(2,1)} fusion(bf16[8,1024,512]{2,1,0:T(8,128)(2,1)} %get-tuple-element.6, s32[1024]{0:T(1024)S(1)} %pad_clamp_fusion), kind=kCustom, calls=%fused_computation | custom fusion | bytes 16777248 | tf_op jit(solution)/shard_map/gather | solution.py:83
  279.0 8.0 %gather_fusion.1 = bf16[8,1024,512]{2,1,0:T(8,128)(2,1)} fusion(bf16[8,1024,512]{2,1,0:T(8,128)(2,1)} %get-tuple-element.7, s32[1024]{0:T(1024)S(1)} %pad_clamp_fusion), kind=kCustom, calls=%fused_computation.1 | custom fusion | bytes 16777248 | tf_op jit(solution)/shard_map/gather | solution.py:83
  287.0 13.6 %maximum_bitcast_fusion = bf16[2048,8,512]{2,0,1:T(8,128)(2,1)} fusion(bf16[8,1024,512]{2,1,0:T(8,128)(2,1)} %gather_fusion.1, bf16[8,1024,512]{2,1,0:T(8,128)(2,1)} %gather_fusion), kind=kLoop, calls=%fused_computation.2 | loop fusion | flops 33554432 | bytes 33554432 | tf_op jit(solution)/shard_map/transpose | solution.py:11
  300.6 21.6 %copy.52 = bf16[2048,8,512]{0,2,1:T(8,128)(2,1)} copy(bf16[2048,8,512]{2,0,1:T(8,128)(2,1)} %maximum_bitcast_fusion) | data formatting | bytes 33554432 | tf_op jit(solution)/shard_map/transpose | solution.py:11
  322.2 10.6 %fusion.6 = bf16[128,2048]{0,1:T(8,128)(2,1)S(1)} fusion(bf16[2048,4096]{0,1:T(8,128)(2,1)} %bitcast.147, bf16[1,1,128,4096]{3,2,1,0:T(8,128)(2,1)} %all-gather.6.cloned.1.call-done, bf16[1,1,1,128,2048]{3,4,2,1,0:T(8,128)(2,1)S(1)} %copy-done.13), kind=kOutput, calls=%fused_computation.11 | convolution fusion | flops 2148270080 | bytes 18874368 | tf_op jit(solution)/shard_map/dot_general | solution.py:67
  354.0 6.1 reshape.244
  366.3 6.2 %reshape.246 = f32[16,128,255]{2,1,0:T(8,128)} reshape(f32[16,32640]{1,0:T(8,128)} %slice.298) | data formatting | bytes 4177920 | tf_op jit(solution)/shard_map/reshape | solution.py:43
  378.8 6.2 reshape.248
  391.4 6.2 reshape.250
  403.8 6.1 reshape.252
  416.1 6.2 reshape.254
  433.2 6.1 reshape.256
  443.7 6.2 reshape.258
  456.2 8.5 %fusion.5 = bf16[128,2048]{1,0:T(8,128)(2,1)S(1)} fusion(bf16[128,4096]{1,0:T(8,128)(2,1)} %all-gather.4.cloned.1.call-done, bf16[2048,4096]{0,1:T(8,128)(2,1)} %bitcast.148, bf16[1,2,1,128,2048]{4,3,2,1,0:T(8,128)(2,1)} %param.7), kind=kOutput, calls=%fused_computation.10 | convolution fusion | flops 2148270080 | bytes 18874368 | tf_op jit(solution)/shard_map/dot_general | solution.py:67
  482.0 6.2 %reshape.260 = f32[16,128,255]{2,1,0:T(8,128)} reshape(f32[16,32640]{1,0:T(8,128)} %slice.312) | data formatting | bytes 4177920 | tf_op jit(solution)/shard_map/reshape | solution.py:43
  494.4 6.1 reshape.262
  506.7 6.4 %reshape.264 = f32[16,128,255]{2,1,0:T(8,128)} reshape(f32[16,32640]{1,0:T(8,128)} %slice.316) | data formatting | bytes 4177920 | tf_op jit(solution)/shard_map/reshape | solution.py:43
  519.4 6.2 reshape.266
  531.8 6.2 reshape.268
  544.2 6.4 %reshape.270 = f32[16,128,255]{2,1,0:T(8,128)} reshape(f32[16,32640]{1,0:T(8,128)} %slice.322) | data formatting | bytes 4177920 | tf_op jit(solution)/shard_map/reshape | solution.py:43
  556.8 6.2 reshape.272
  566.3 4.6 reshape.274
  576.5 33.9 %reduce-scatter.4.cloned.1.call-done = f32[16,128]{1,0:T(8,128)} async-done(((f32[128,128]{1,0:T(8,128)}), f32[16,128]{1,0:T(8,128)}) %reduce-scatter.4.cloned.1.call-update) | async-done | bytes 8208
  (172 shorter events, 171.6 us)
Async XLA Ops:
  7.2 150.7 %copy-start.14 = (bf16[1,128,128]{2,1,0:T(8,128)(2,1)S(1)}, bf16[1,128,128]{2,1,0:T(8,128)(2,1)}, u32[]{:S(2)}) copy-start(bf16[1,128,128]{2,1,0:T(8,128)(2,1)} %param.11) | copy-start | bytes 98308
  7.2 315.1 %all-gather.6.cloned.1.call-start = ((), (), s32[]{:S(2)}) async-start(), calls=%async_computation.2 | async-start | bytes 1572864 | tf_op jit(solution)/shard_map/all_gather | solution.py:64
  7.2 51.8 %collective-permute-start = (bf16[2048,512]{1,0:T(8,128)(2,1)}, bf16[2048,512]{1,0:T(8,128)(2,1)S(1)}, u32[]{:S(2)}, u32[]{:S(2)}) collective-permute-start(bf16[2048,512]{1,0:T(8,128)(2,1)} %bitcast.208), channel_id=1, source_target_pairs={{0,2},{2,4},{4,6},{6,8},{8,10},{10,12},{12,14},{14,0},{1,3},{3,5},... | collective-permute-start | bytes 6291464 | tf_op jit(solution)/shard_map/ppermute | solution.py:77
  59.0 48.0 %collective-permute-start.1 = (bf16[2048,512]{1,0:T(8,128)(2,1)S(1)}, bf16[2048,512]{1,0:T(8,128)(2,1)S(1)}, u32[]{:S(2)}, u32[]{:S(2)}) collective-permute-start(bf16[2048,512]{1,0:T(8,128)(2,1)S(1)} %collective-permute-done), channel_id=1, source_target_pairs={{0,2},{2,4},{4,6},{6,8},{8,10},{10,12},{12,14},{14,0},{1,3},{3,5},... | collective-permute-start | bytes 6291464 | tf_op jit(solution)/shard_map/ppermute | solution.py:77
  59.0 49.3 %collective-permute-start.4 = (bf16[2048,512]{1,0:T(8,128)(2,1)}, bf16[2048,512]{1,0:T(8,128)(2,1)}, u32[]{:S(2)}, u32[]{:S(2)}) collective-permute-start(bf16[2048,512]{1,0:T(8,128)(2,1)} %bitcast.209), channel_id=1, source_target_pairs={{2,0},{4,2},{6,4},{8,6},{10,8},{12,10},{14,12},{0,14},{3,1},{5,3},... | collective-permute-start | bytes 6291464 | tf_op jit(solution)/shard_map/ppermute | solution.py:80
  107.0 1.3 copy-start.10
  108.3 47.2 %collective-permute-start.2 = (bf16[2048,512]{1,0:T(8,128)(2,1)S(1)}, bf16[2048,512]{1,0:T(8,128)(2,1)}, u32[]{:S(2)}, u32[]{:S(2)}) collective-permute-start(bf16[2048,512]{1,0:T(8,128)(2,1)S(1)} %collective-permute-done.1), channel_id=1, source_target_pairs={{0,2},{2,4},{4,6},{6,8},{8,10},{10,12},{12,14},{14,0},{1,3},{3,5},... | collective-permute-start | bytes 6291464 | tf_op jit(solution)/shard_map/ppermute | solution.py:77
  108.3 110.2 %collective-permute-start.5 = (bf16[2048,512]{1,0:T(8,128)(2,1)}, bf16[2048,512]{1,0:T(8,128)(2,1)}, u32[]{:S(2)}, u32[]{:S(2)}) collective-permute-start(bf16[2048,512]{1,0:T(8,128)(2,1)} %collective-permute-done.4), channel_id=1, source_target_pairs={{2,0},{4,2},{6,4},{8,6},{10,8},{12,10},{14,12},{0,14},{3,1},{5,3},... | collective-permute-start | bytes 6291464 | tf_op jit(solution)/shard_map/ppermute | solution.py:80
  155.5 66.7 %collective-permute-start.3 = (bf16[2048,512]{1,0:T(8,128)(2,1)}, bf16[2048,512]{1,0:T(8,128)(2,1)}, u32[]{:S(2)}, u32[]{:S(2)}) collective-permute-start(bf16[2048,512]{1,0:T(8,128)(2,1)} %collective-permute-done.2), channel_id=1, source_target_pairs={{0,2},{2,4},{4,6},{6,8},{8,10},{10,12},{12,14},{14,0},{1,3},{3,5},... | collective-permute-start | bytes 6291464 | tf_op jit(solution)/shard_map/ppermute | solution.py:77
  155.6 300.6 %all-gather.4.cloned.1.call-start = ((), (), s32[]{:S(2)}) async-start(), calls=%async_computation.1 | async-start | bytes 1572864 | tf_op jit(solution)/shard_map/all_gather | solution.py:64
  181.3 29.6 %copy-start.1 = (bf16[1,2,1,128,2048]{4,3,2,1,0:T(8,128)(2,1)S(1)}, bf16[1,2,1,128,2048]{4,3,2,1,0:T(8,128)(2,1)}, u32[]{:S(2)}) copy-start(bf16[1,2,1,128,2048]{4,3,2,1,0:T(8,128)(2,1)} %param.8) | copy-start | bytes 3145732
  218.6 46.2 %collective-permute-start.6 = (bf16[2048,512]{1,0:T(8,128)(2,1)}, bf16[2048,512]{1,0:T(8,128)(2,1)S(1)}, u32[]{:S(2)}, u32[]{:S(2)}) collective-permute-start(bf16[2048,512]{1,0:T(8,128)(2,1)} %collective-permute-done.5), channel_id=1, source_target_pairs={{2,0},{4,2},{6,4},{8,6},{10,8},{12,10},{14,12},{0,14},{3,1},{5,3},... | collective-permute-start | bytes 6291464 | tf_op jit(solution)/shard_map/ppermute | solution.py:80
  224.0 2.2 copy-start.11
  226.4 1.6 copy-start.9
  300.6 21.6 %copy-start.13 = (bf16[1,1,1,128,2048]{3,4,2,1,0:T(8,128)(2,1)S(1)}, bf16[1,1,1,128,2048]{3,4,2,1,0:T(8,128)(2,1)}, u32[]{:S(2)}) copy-start(bf16[1,1,1,128,2048]{3,4,2,1,0:T(8,128)(2,1)} %copy.63) | copy-start | bytes 1572868
  332.9 10.1 %slice-start = ((s8[8388608]{0:T(1024)(128)(4,1)}), s8[4194304]{0:T(1024)(128)(4,1)S(1)}, s32[]{:S(2)}) async-start(s8[8388608]{0:T(1024)(128)(4,1)} %bitcast.149), calls=%async_computation.4 | async-start | bytes 8388608
  338.0 5.0 slice-start.1
  345.3 1.3 copy-start.4
  346.6 4.6 copy-start
  349.2 78.5 %collective-permute-start.7 = (bf16[128,2048]{1,0:T(8,128)(2,1)}, bf16[128,2048]{1,0:T(8,128)(2,1)S(1)}, u32[]{:S(2)}, u32[]{:S(2)}) collective-permute-start(bf16[128,2048]{1,0:T(8,128)(2,1)} %fusion.10), channel_id=1, source_target_pairs={{16,0},{32,16},{48,32},{64,48},{80,64},{96,80},{112,96},{128,112},... | collective-permute-start | bytes 1572872 | tf_op jit(solution)/shard_map/ppermute | solution.py:17
  427.6 0.8 copy-start.8
  428.4 182.0 %reduce-scatter.4.cloned.1.call-start = ((), (), s32[]{:S(2)}) async-start(), calls=%async_computation.3 | async-start | bytes 73728
  449.9 5.3 copy-start.2
  449.9 5.3 copy-start.5
  451.2 4.0 copy-start.6
  465.3 10.7 %slice-start.2 = ((s8[8388608]{0:T(1024)(128)(4,1)}), s8[4194304]{0:T(1024)(128)(4,1)S(1)}, s32[]{:S(2)}) async-start(s8[8388608]{0:T(1024)(128)(4,1)} %bitcast.151), calls=%async_computation.6 | async-start | bytes 8388608
  470.4 5.6 slice-start.3
  566.3 7.5 %copy-start.7 = (f32[128,16,128]{2,1,0:T(8,128)S(1)}, f32[128,16,128]{2,1,0:T(8,128)}, u32[]{:S(2)}) copy-start(f32[128,16,128]{2,1,0:T(8,128)} %fusion) | copy-start | bytes 3145732
  570.9 3.2 copy-start.3
  574.1 1.3 copy-start.12
Sparse Core Ops, SparseCore 0:
  155.7 26.9 all-gather.5
  428.6 27.1 all-gather.3
  573.9 36.5 reduce-scatter.3
